TPU v7x, 512 devices: a whole 4x4x16 slice. The times are simulated.
512 devices in a mesh: ep: 128 (over z, y, core), dp: 4 (over x).
Axes of the slice: x: 4, y: 4, z: 16, core: 2. Of those that a mesh axis runs over, the one named last changes fastest.
Arguments:
- out_grads: bfloat16 [65536, 2048], P(('ep', 'dp')), may hold values from -40 to 40
- hidden_acts: bfloat16 [65536, 512], P(('ep', 'dp')), may hold values from -20 to 20
- routing: int32 [65536, 1], P(('ep', 'dp')), may hold values from 0 to 95, as said below
- replica_pick: int32 [65536], P(('ep', 'dp')), may hold values from 0 to 3
- master_weights: float32 [128, 2048, 512], P('ep', 'dp'), may hold values from -0.25 to 0.25
- current_slots: int32 [128], replicated, may hold values from 0 to 95, as said below
- next_slots: int32 [128], replicated, may hold values from 0 to 95, as said below
Outputs:
- input_grads: float32 [65536, 512], P(('ep', 'dp'))
- moved_weights: float32 [128, 2048, 512], P('ep', 'dp')
- moved_updates: float32 [128, 2048, 512], P('ep', 'dp')
Inputs may be any that keep to these rules, and one draw needn't show every extreme that they name: `routing`: the rows of one device name each expert at most 2 times; the experts held by two slots now are named exactly 2 times by the rows of every device. `current_slots`: every expert below 96 is held by one or two slots. `next_slots`: every expert below 96 is held by at least one slot.
All inputs are finite; a program needn't handle non-finite values.
Results may differ from a plain program's by a relative error of at most 0.0029.
Values may be sent and summed in bfloat16 or wider, within the bound.
A program may use at most 64 MiB of HBM per device.

v0:
```python
import jax
import jax.numpy as jnp
from jax import lax
from jax.experimental import pallas as pl
from jax.experimental.pallas import tpu as pltpu
from jax.sharding import PartitionSpec as P

POLY_FIRST = 3.4445
POLY_SECOND = -4.775
POLY_THIRD = 2.0315
LEARNING_RATE = 0.02
UPDATE_SCALE = 0.2
EPSILON = 1e-07
PRECISE = lax.Precision.HIGHEST
BF16 = jnp.bfloat16
F32 = jnp.float32
MESH = pl.DeviceIdType.MESH
N_EP = 128
N_DP = 4
N_Z = 16
N_YC = 8
ROWS = 2 * N_EP
WIDE = 512
FLAG = 128
CHUNKS = 2
CHUNK = WIDE // CHUNKS


def span(start, size):
    return pl.ds(pl.multiple_of(start, size), size)


def wait_bytes(ref, sem):
    pltpu.make_async_copy(ref, ref, sem).wait()


def greet(z, yc, col):
    barrier = pltpu.get_barrier_semaphore()
    for k in range(1, N_Z):
        peer = lax.rem(z + k, N_Z) * N_YC + yc
        pl.semaphore_signal(barrier, inc=1, device_id={"ep": peer}, device_id_type=MESH)
    for k in range(1, N_YC):
        peer = z * N_YC + lax.rem(yc + k, N_YC)
        pl.semaphore_signal(barrier, inc=1, device_id={"ep": peer}, device_id_type=MESH)
    for k in range(1, N_DP):
        peer = lax.rem(col + k, N_DP)
        pl.semaphore_signal(barrier, inc=1, device_id={"dp": peer}, device_id_type=MESH)
    pl.semaphore_wait(barrier, N_Z - 1 + N_YC - 1 + N_DP - 1)


def send(src, dst, sems, where):
    pltpu.make_async_remote_copy(
        src_ref=src,
        dst_ref=dst,
        send_sem=sems.at[0],
        recv_sem=sems.at[1],
        device_id=where,
        device_id_type=MESH,
    ).start()


def turn_rows(values, outer, inner):
    shape = (ROWS, ROWS)
    row = lax.broadcasted_iota(jnp.int32, shape, 0)
    column = lax.broadcasted_iota(jnp.int32, shape, 1)
    o = row // (2 * inner)
    i = lax.rem(row, 2 * inner) // 2
    p = lax.rem(row, 2)
    onehot = (column == i * (2 * outer) + o * 2 + p).astype(F32).astype(BF16)
    return jnp.dot(onehot, values, preferred_element_type=F32).astype(BF16)


def exact(left, right):
    return jnp.dot(left, right, precision=PRECISE, preferred_element_type=F32)


def pick(onehot, values):
    return jnp.dot(onehot, values, preferred_element_type=F32).astype(BF16)


def iota(shape, dimension):
    return lax.broadcasted_iota(jnp.int32, shape, dimension)


def count(mask, axis):
    return jnp.sum(mask.astype(F32), axis=axis, keepdims=True)


def plan(named_ref, pick_ref, now_ref, next_ref):
    square = (N_EP, N_EP)
    upper, lower = iota(square, 0), iota(square, 1)

    def column(row):
        return jnp.sum(jnp.where(upper == lower, row, 0.0), axis=1, keepdims=True)

    named = named_ref[...].astype(F32)
    now = now_ref[...].astype(F32)
    later = next_ref[...].astype(F32)
    now_column = column(now)
    place = count((column(named) == named) & (upper < lower), 0)
    holders = count(now_column == named, 0)
    second = jnp.where(
        (holders == 2.0) & (lax.rem(pick_ref[...], 2) == 1), 1.0, 0.0
    )
    rank_now = count((now_column == now) & (lower < upper), 1)
    rank_next = count((column(later) == later) & (upper < lower), 0)
    turned = upper == lax.rem(lower, N_Z) * N_YC + lower // N_Z
    now_turned = jnp.sum(jnp.where(turned, now_column, 0.0), axis=0, keepdims=True)
    rank_turned = jnp.sum(jnp.where(turned, rank_now, 0.0), axis=0, keepdims=True)
    tall = (ROWS, N_EP)
    row, lane = iota(tall, 0), iota(tall, 1)
    own = lane == lax.rem(row // 2, N_Z) * N_YC + row // (2 * N_Z)
    wanted = jnp.sum(jnp.where(own, later, 0.0), axis=1, keepdims=True)
    leads = jnp.sum(jnp.where(own, rank_next, 0.0), axis=1, keepdims=True) == 0.0
    pair = lax.rem(row, 2).astype(F32)
    to_slot = jnp.where((wanted == named) & (place == pair), 1.0, 0.0)
    back = jnp.where(leads, to_slot, 0.0)
    flag = jnp.sum(to_slot * second, axis=1, keepdims=True)
    hop = jnp.where((wanted == now_turned) & (rank_turned == pair), 1.0, 0.0)
    return to_slot.astype(BF16), back.astype(BF16), flag, hop.astype(BF16)


def kernel(
    og_ref, ha_ref, named_ref, pick_ref, weight_ref, now_ref, next_ref,
    out_ref, mov_ref, upd_ref,
    wb, wz, wp, wide, chosen, pay, hop, w01,
    ogs, ogx, ogy, ogp, ogz, has, hy, hp, hg, back,
    lhs, grad, gram, gram_got, poly, turn,
    part_send, part_got, total, sums, bz, bp, ret,
    wz_sem, wy_sem, hopy_sem, hopz_sem, x_sem, y_sem, z_sem, hy_sem, hz_sem, hx_sem,
    g_sem, a_sem, p_sem, bz_sem, by_sem,
):
    me = lax.axis_index("ep")
    col = lax.axis_index("dp")
    z = me // N_YC
    yc = lax.rem(me, N_YC)

    def over_z(body):
        def step(k, carry):
            peer = lax.rem(z + k, N_Z)
            body(peer, {"ep": peer * N_YC + yc})
            return carry

        lax.fori_loop(1, N_Z, step, 0)

    def over_yc(body):
        def step(k, carry):
            peer = lax.rem(yc + k, N_YC)
            body(peer, {"ep": z * N_YC + peer})
            return carry

        lax.fori_loop(1, N_YC, step, 0)

    my16, my32z, my32y = span(z * 16, 16), span(z * 32, 32), span(yc * 32, 32)
    my_half, my_cols = span((yc // 4) * 16, 16), span(lax.rem(yc, 4) * 128, 128)

    greet(z, yc, col)

    wb[...] = weight_ref[...].astype(BF16)
    over_z(lambda peer, there: send(wb.at[span(peer * 32, 32), :], wz.at[z], wz_sem, there))
    wz[z] = wb[my32z, :]

    to_slot, leading, flag, hop_onehot = plan(named_ref, pick_ref, now_ref, next_ref)
    back[...] = leading
    ogs[...] = pick(to_slot, og_ref[...])
    for k in range(1, N_DP):
        peer = lax.rem(col + k, N_DP)
        send(ogs.at[:, span(peer * WIDE, WIDE)], ogx.at[col], x_sem, {"dp": peer})
    has[:, :WIDE] = pick(to_slot, ha_ref[...])
    has[:, WIDE:] = jnp.broadcast_to(flag, (ROWS, FLAG)).astype(BF16)
    over_yc(
        lambda peer, there: send(has.at[span(peer * 32, 32), :], hy.at[my32y, :], hy_sem, there)
    )
    hy[my32y, :] = has[my32y, :]
    ogx[col] = ogs[:, span(col * WIDE, WIDE)]

    wait_bytes(hy.at[pl.ds(0, 32 * (N_YC - 1)), :], hy_sem.at[1])
    hp[...] = turn_rows(hy[...], N_Z, N_YC)
    over_z(
        lambda peer, there: send(
            hp.at[span(peer * 16, 16), :], hg.at[col, my16, :], hz_sem, there
        )
    )
    hg[col, my16, :] = hp[my16, :]

    wait_bytes(ogx.at[pl.ds(0, N_DP - 1)], x_sem.at[1])
    over_yc(
        lambda peer, there: send(
            ogx.at[:, span(peer * 32, 32), :], ogy.at[:, my32y, :], y_sem, there
        )
    )
    ogy[:, my32y, :] = ogx[:, my32y, :]

    wait_bytes(wz.at[pl.ds(0, N_Z - 1)], wz_sem.at[1])
    over_yc(
        lambda peer, there: send(
            wz.at[:, span((peer // 4) * 16, 16), span(lax.rem(peer, 4) * 128, 128)],
            wp.at[yc], wy_sem, there,
        )
    )
    wp[yc] = wz[:, my_half, my_cols]

    wait_bytes(ogy.at[:, pl.ds(0, 32 * (N_YC - 1)), :], y_sem.at[1])
    for g in range(N_DP):
        ogp[g] = turn_rows(ogy[g], N_Z, N_YC)
    over_z(
        lambda peer, there: send(
            ogp.at[:, span(peer * 16, 16), :], ogz.at[:, my16, :], z_sem, there
        )
    )
    ogz[:, my16, :] = ogp[:, my16, :]

    wait_bytes(wp.at[pl.ds(0, N_YC - 1)], wy_sem.at[1])
    wide[...] = wp[...].reshape(N_EP * 16, 128).astype(F32)
    for j in range(16):
        piece = wide[pl.ds(j, N_EP, stride=16), :].astype(BF16)
        chosen[pl.ds(j, ROWS, stride=16), :] = jnp.dot(
            hop_onehot, piece, preferred_element_type=F32
        )
    pay[...] = chosen[...].astype(BF16).reshape(N_YC, N_Z, 2, 16, 128)
    over_yc(
        lambda peer, there: send(
            pay.at[peer], hop.at[:, :, my_half, my_cols], hopy_sem, there
        )
    )
    hop[:, :, my_half, my_cols] = pay[yc]

    wait_bytes(hp.at[pl.ds(0, 16 * (N_Z - 1)), :], hz_sem.at[1])
    for k in range(1, N_DP):
        peer = lax.rem(col + k, N_DP)
        send(hg.at[col], hg.at[col], hx_sem, {"dp": peer})

    wait_bytes(pay.at[pl.ds(0, N_YC - 1)], hopy_sem.at[1])
    over_z(lambda peer, there: send(hop.at[peer], w01.at[:, my32z, :], hopz_sem, there))
    w01[:, my32z, :] = hop[z]

    wait_bytes(hg.at[pl.ds(0, N_DP - 1)], hx_sem.at[1])
    wait_bytes(ogz.at[:, pl.ds(0, 16 * (N_Z - 1)), :], z_sem.at[1])
    acts = hg[:, :, :WIDE].reshape(N_DP * ROWS, WIDE)
    for c in range(0, WIDE, 256):
        grad[c : c + 256, :] = lax.dot_general(
            ogz[:, :, c : c + 256].reshape(N_DP * ROWS, 256),
            acts,
            (((0,), (0,)), ((), ())),
            preferred_element_type=F32,
        )
    for c in range(0, WIDE, 128):
        gram[c : c + 128, :] = exact(grad[:, c : c + 128].T, grad[...])

    for k in range(1, N_DP):
        peer = lax.rem(col + k, N_DP)
        send(gram.at[span(peer * 128, 128), :], gram_got.at[k - 1], g_sem.at[k - 1], {"dp": peer})
    for g in range(N_DP):
        second = jnp.concatenate([hg[g, :, WIDE:]] * (WIDE // FLAG), axis=1).astype(F32)
        rows = ogz[g].astype(F32)
        lhs[g, :, :WIDE] = (rows * (1.0 - second)).astype(BF16)
        lhs[g, :, WIDE:] = (rows * second).astype(BF16)
    share = gram[span(col * 128, 128), :]
    for k in range(1, N_DP):
        wait_bytes(gram_got.at[k - 1], g_sem.at[k - 1, 1])
        share = share + gram_got[k - 1]
    poly[span(col * 128, 128), :] = share
    for k in range(1, N_DP):
        peer = lax.rem(col + k, N_DP)
        send(
            poly.at[span(col * 128, 128), :], poly.at[span(col * 128, 128), :], a_sem,
            {"dp": peer},
        )
    for k in range(1, N_DP):
        wait_bytes(gram_got.at[k - 1], g_sem.at[k - 1, 0])
    wait_bytes(gram_got, a_sem.at[1])
    wait_bytes(gram_got, a_sem.at[0])

    eye = jnp.where(iota((WIDE, WIDE), 0) == iota((WIDE, WIDE), 1), 1.0, 0.0)
    square = jnp.sum(poly[...] * eye, keepdims=True)
    scale = 1.0 / (jnp.sqrt(square) + EPSILON)
    a1 = poly[...] * scale * scale
    q1 = POLY_FIRST * eye + POLY_SECOND * a1 + POLY_THIRD * exact(a1, a1)
    a2 = exact(exact(q1, a1), q1)
    q2 = POLY_FIRST * eye + POLY_SECOND * a2 + POLY_THIRD * exact(a2, a2)
    turn[...] = exact(q1, q2) * (scale * (UPDATE_SCALE * (N_DP * WIDE) ** 0.5))
    upd_ref[...] = exact(grad[...], turn[...])

    wait_bytes(hop.at[pl.ds(0, N_Z - 1)], hopz_sem.at[1])
    for c in range(CHUNKS):
        lanes = pl.ds(c * CHUNK, CHUNK)
        weight = w01[:, :, lanes].reshape(2 * WIDE, CHUNK)
        for k in (1, 2, 3, 0):
            g = lax.rem(col + k, N_DP)
            product = jnp.dot(lhs[g], weight, preferred_element_type=F32)
            if k:
                part_send[c, k - 1] = product.astype(BF16)
                send(part_send.at[c, k - 1], part_got.at[c, k - 1], p_sem.at[c], {"dp": g})
            else:
                total[c] = product
    for c in range(CHUNKS):
        wait_bytes(part_got.at[c], p_sem.at[c, 1])
        got = part_got[c].astype(F32)
        sums[c] = (total[c] + got[0] + got[1] + got[2]).astype(BF16)
        over_z(
            lambda peer, there: send(
                sums.at[c, span(peer * 16, 16), :], bz.at[c, my16, :], bz_sem.at[c], there
            )
        )
        bz[c, my16, :] = sums[c, my16, :]
    mov_ref[...] = w01[0].astype(F32) - LEARNING_RATE * upd_ref[...]
    for c in range(CHUNKS):
        wait_bytes(bz.at[c, pl.ds(0, 16 * (N_Z - 1)), :], bz_sem.at[c, 1])
        bp[c] = turn_rows(bz[c], N_YC, N_Z)
        over_yc(
            lambda peer, there: send(
                bp.at[c, span(peer * 32, 32), :], ret.at[c, my32y, :], by_sem.at[c], there
            )
        )
        ret[c, my32y, :] = bp[c, my32y, :]
    for c in range(CHUNKS):
        wait_bytes(ret.at[c, pl.ds(0, 32 * (N_YC - 1)), :], by_sem.at[c, 1])
        out_ref[:, pl.ds(c * CHUNK, CHUNK)] = lax.dot_general(
            back[...], ret[c], (((0,), (0,)), ((), ())), preferred_element_type=F32
        )

    for c in range(CHUNKS):
        wait_bytes(part_got.at[c], p_sem.at[c, 0])
        wait_bytes(bz.at[c, pl.ds(0, 16 * (N_Z - 1)), :], bz_sem.at[c, 0])
        wait_bytes(ret.at[c, pl.ds(0, 32 * (N_YC - 1)), :], by_sem.at[c, 0])
    wait_bytes(wz.at[pl.ds(0, N_Z - 1)], wz_sem.at[0])
    wait_bytes(wp.at[pl.ds(0, N_YC - 1)], wy_sem.at[0])
    wait_bytes(pay.at[pl.ds(0, N_YC - 1)], hopy_sem.at[0])
    wait_bytes(hop.at[pl.ds(0, N_Z - 1)], hopz_sem.at[0])
    wait_bytes(ogx.at[pl.ds(0, N_DP - 1)], x_sem.at[0])
    wait_bytes(ogy.at[:, pl.ds(0, 32 * (N_YC - 1)), :], y_sem.at[0])
    wait_bytes(ogz.at[:, pl.ds(0, 16 * (N_Z - 1)), :], z_sem.at[0])
    wait_bytes(hy.at[pl.ds(0, 32 * (N_YC - 1)), :], hy_sem.at[0])
    wait_bytes(hp.at[pl.ds(0, 16 * (N_Z - 1)), :], hz_sem.at[0])
    wait_bytes(hg.at[pl.ds(0, N_DP - 1)], hx_sem.at[0])


def call(kernel, outs, scratch, semaphores, collective_id, *args):
    vmem = pl.BlockSpec(memory_space=pltpu.VMEM)
    return pl.pallas_call(
        kernel,
        out_shape=[jax.ShapeDtypeStruct(*o) for o in outs],
        in_specs=[vmem] * len(args),
        out_specs=[vmem] * len(outs),
        scratch_shapes=[pltpu.VMEM(*s) for s in scratch]
        + [pltpu.SemaphoreType.DMA(s) for s in semaphores],
        compiler_params=pltpu.CompilerParams(
            collective_id=collective_id, has_side_effects=True, vmem_limit_bytes=48 * 2**20
        ),
    )(*args)


def per_device(
    out_grads, hidden_acts, routing, replica_pick, master_weights, current_slots, next_slots
):
    wide_acts = WIDE + FLAG
    input_grads, moved_weight, update = call(
        kernel,
        [((N_EP, WIDE), F32), ((WIDE, WIDE), F32), ((WIDE, WIDE), F32)],
        [
            ((WIDE, WIDE), BF16),
            ((N_Z, 32, WIDE), BF16),
            ((N_YC, N_Z, 16, 128), BF16),
            ((N_EP * 16, 128), F32),
            ((ROWS * 16, 128), F32),
            ((N_YC, N_Z, 2, 16, 128), BF16),
            ((N_Z, 2, 32, WIDE), BF16),
            ((2, WIDE, WIDE), BF16),
            ((ROWS, N_DP * WIDE), BF16),
            ((N_DP, ROWS, WIDE), BF16),
            ((N_DP, ROWS, WIDE), BF16),
            ((N_DP, ROWS, WIDE), BF16),
            ((N_DP, ROWS, WIDE), BF16),
            ((ROWS, wide_acts), BF16),
            ((ROWS, wide_acts), BF16),
            ((ROWS, wide_acts), BF16),
            ((N_DP, ROWS, wide_acts), BF16),
            ((ROWS, N_EP), BF16),
            ((N_DP, ROWS, 2 * WIDE), BF16),
            ((WIDE, WIDE), F32),
            ((WIDE, WIDE), F32),
            ((3, 128, WIDE), F32),
            ((WIDE, WIDE), F32),
            ((WIDE, WIDE), F32),
            ((CHUNKS, 3, ROWS, CHUNK), BF16),
            ((CHUNKS, 3, ROWS, CHUNK), BF16),
            ((CHUNKS, ROWS, CHUNK), F32),
            ((CHUNKS, ROWS, CHUNK), BF16),
            ((CHUNKS, ROWS, CHUNK), BF16),
            ((CHUNKS, ROWS, CHUNK), BF16),
            ((CHUNKS, ROWS, CHUNK), BF16),
        ],
        [(2,)] * 10 + [(3, 2), (2,)] + [(CHUNKS, 2)] * 3,
        0,
        out_grads,
        hidden_acts,
        routing.reshape(1, N_EP),
        replica_pick.reshape(1, N_EP),
        master_weights[0],
        current_slots.reshape(1, N_EP),
        next_slots.reshape(1, N_EP),
    )
    return (input_grads, moved_weight[None], update[None])


def solution(mesh):
    placed = (
        P(("ep", "dp"), None),
        P(("ep", "dp"), None),
        P(("ep", "dp"), None),
        P(("ep", "dp")),
        P("ep", "dp", None),
        P(),
        P(),
    )
    return jax.shard_map(
        per_device,
        mesh=mesh,
        in_specs=placed,
        out_specs=(P(("ep", "dp"), None), P("ep", "dp", None), P("ep", "dp", None)),
        check_vma=False,
    )
```

profile of v0, /device:TPU:1, one launch (start us, length us, event | category | flops | bytes accessed | tf_op | source)
XLA Modules:
  0.0 181.6 jit_solution(15908799073540131622)
XLA Ops:
  0.6 0.0 copy-start.6
  0.6 0.0 copy-start.3
  0.7 0.0 copy-start.4
  0.7 0.0 copy-start.5
  0.7 0.6 copy-done.6
  1.3 0.0 copy-done.3
  1.3 0.0 copy-done.4
  1.3 0.0 copy-done.5
  1.3 0.0 copy-start
  1.3 1.2 copy-done
  2.6 0.0 copy-start.1
  2.6 1.0 copy-done.1
  3.6 0.0 copy-start.2
  3.6 0.9 copy-done.2
  4.5 174.4 %shard_map.94 = (f32[128,512]{1,0:T(8,128)S(1)}, f32[512,512]{1,0:T(8,128)S(1)}, f32[512,512]{1,0:T(8,128)S(1)}) custom-call(bf16[128,2048]{1,0:T(8,128)(2,1)S(1)} %copy-done.1, bf16[128,512]{1,0:T(8,128)(2,1)S(1)} %copy-done.2, s32[1,128]{1,0:T(1,128)S(1)} %bitcast.10, s32[1,128]{1,0:T(1,128)S(1)} %bitcast.11, f32[512,512]{1,0:T(8,128)S(1)} %bitcast.7, ...), custom_call_target="tpu_custom_call" | custom-call | tf_op jit(solution)/shard_map/pallas_call | solution.py:340
  178.9 0.7 copy.13
  179.6 1.0 copy.14
  180.6 1.0 copy.15
Async XLA Ops:
  0.6 0.7 copy-start.6
  0.6 0.7 copy-start.3
  0.7 0.7 copy-start.4
  0.7 0.7 copy-start.5
  1.3 1.2 copy-start
  2.6 1.0 copy-start.1
  3.6 0.9 copy-start.2
where the time goes:
time: 182 us
  Pallas kernels  174 us (96%)
  local copies, waits for them, and re-layouts  6.48 us (4%)
    pallas_call x1, Pallas kernels, call(): pl.pallas_call(kernel, out_shape=[jax.ShapeDtypeStruct(*o) for o in outs]...  174 us
    unnamed x17, local copies, waits for them, and re-layouts  6.48 us

commit v1 on v0

--- a/solution.py
+++ b/solution.py
@@ -22,7 +22,7 @@
 ROWS = 2 * N_EP
 WIDE = 512
 FLAG = 128
-CHUNKS = 2
+CHUNKS = 4
 CHUNK = WIDE // CHUNKS
 
 
@@ -45,7 +45,6 @@
     for k in range(1, N_DP):
         peer = lax.rem(col + k, N_DP)
         pl.semaphore_signal(barrier, inc=1, device_id={"dp": peer}, device_id_type=MESH)
-    pl.semaphore_wait(barrier, N_Z - 1 + N_YC - 1 + N_DP - 1)
 
 
 def send(src, dst, sems, where):
@@ -86,21 +85,21 @@
     return jnp.sum(mask.astype(F32), axis=axis, keepdims=True)
 
 
-def plan(named_ref, pick_ref, now_ref, next_ref):
+def plan(named, picked, now, later):
     square = (N_EP, N_EP)
     upper, lower = iota(square, 0), iota(square, 1)
 
     def column(row):
         return jnp.sum(jnp.where(upper == lower, row, 0.0), axis=1, keepdims=True)
 
-    named = named_ref[...].astype(F32)
-    now = now_ref[...].astype(F32)
-    later = next_ref[...].astype(F32)
+    named = named.astype(F32)
+    now = now.astype(F32)
+    later = later.astype(F32)
     now_column = column(now)
     place = count((column(named) == named) & (upper < lower), 0)
     holders = count(now_column == named, 0)
     second = jnp.where(
-        (holders == 2.0) & (lax.rem(pick_ref[...], 2) == 1), 1.0, 0.0
+        (holders == 2.0) & (lax.rem(picked, 2) == 1), 1.0, 0.0
     )
     rank_now = count((now_column == now) & (lower < upper), 1)
     rank_next = count((column(later) == later) & (upper < lower), 0)
@@ -123,12 +122,13 @@
 def kernel(
     og_ref, ha_ref, named_ref, pick_ref, weight_ref, now_ref, next_ref,
     out_ref, mov_ref, upd_ref,
+    og_in, ha_in, weight_in, tables, home, moved, updated,
     wb, wz, wp, wide, chosen, pay, hop, w01,
     ogs, ogx, ogy, ogp, ogz, has, hy, hp, hg, back,
     lhs, grad, gram, gram_got, poly, turn,
     part_send, part_got, total, sums, bz, bp, ret,
     wz_sem, wy_sem, hopy_sem, hopz_sem, x_sem, y_sem, z_sem, hy_sem, hz_sem, hx_sem,
-    g_sem, a_sem, p_sem, bz_sem, by_sem,
+    g_sem, a_sem, p_sem, bz_sem, by_sem, in_sem, out_sem,
 ):
     me = lax.axis_index("ep")
     col = lax.axis_index("dp")
@@ -137,7 +137,8 @@
 
     def over_z(body):
         def step(k, carry):
-            peer = lax.rem(z + k, N_Z)
+            away = jnp.where(lax.rem(k, 2) == 1, (k + 1) // 2, N_Z - k // 2)
+            peer = lax.rem(z + away, N_Z)
             body(peer, {"ep": peer * N_YC + yc})
             return carry
 
@@ -154,19 +155,29 @@
     my16, my32z, my32y = span(z * 16, 16), span(z * 32, 32), span(yc * 32, 32)
     my_half, my_cols = span((yc // 4) * 16, 16), span(lax.rem(yc, 4) * 128, 128)
 
+    loads = [(weight_ref, weight_in), (og_ref, og_in), (ha_ref, ha_in)]
+    loads += [(r, tables.at[i]) for i, r in enumerate((named_ref, pick_ref, now_ref, next_ref))]
+    loads = [pltpu.make_async_copy(*pair, in_sem.at[i]) for i, pair in enumerate(loads)]
+    for load in loads:
+        load.start()
+    chunks = [pl.ds(c * CHUNK, CHUNK) for c in range(CHUNKS)]
     greet(z, yc, col)
 
-    wb[...] = weight_ref[...].astype(BF16)
+    loads[0].wait()
+    wb[...] = weight_in[...].astype(BF16)
+    pl.semaphore_wait(pltpu.get_barrier_semaphore(), N_Z - 1 + N_YC - 1 + N_DP - 1)
     over_z(lambda peer, there: send(wb.at[span(peer * 32, 32), :], wz.at[z], wz_sem, there))
     wz[z] = wb[my32z, :]
 
-    to_slot, leading, flag, hop_onehot = plan(named_ref, pick_ref, now_ref, next_ref)
+    for load in loads[1:]:
+        load.wait()
+    to_slot, leading, flag, hop_onehot = plan(*[tables[i] for i in range(4)])
     back[...] = leading
-    ogs[...] = pick(to_slot, og_ref[...])
+    ogs[...] = pick(to_slot, og_in[...])
     for k in range(1, N_DP):
         peer = lax.rem(col + k, N_DP)
         send(ogs.at[:, span(peer * WIDE, WIDE)], ogx.at[col], x_sem, {"dp": peer})
-    has[:, :WIDE] = pick(to_slot, ha_ref[...])
+    has[:, :WIDE] = pick(to_slot, ha_in[...])
     has[:, WIDE:] = jnp.broadcast_to(flag, (ROWS, FLAG)).astype(BF16)
     over_yc(
         lambda peer, there: send(has.at[span(peer * 32, 32), :], hy.at[my32y, :], hy_sem, there)
@@ -231,8 +242,48 @@
         send(hg.at[col], hg.at[col], hx_sem, {"dp": peer})
 
     wait_bytes(pay.at[pl.ds(0, N_YC - 1)], hopy_sem.at[1])
-    over_z(lambda peer, there: send(hop.at[peer], w01.at[:, my32z, :], hopz_sem, there))
+    for lanes, sem in zip(chunks, range(CHUNKS)):
+        over_z(
+            lambda peer, there: send(
+                hop.at[peer, :, :, lanes], w01.at[:, my32z, lanes], hopz_sem.at[sem], there
+            )
+        )
     w01[:, my32z, :] = hop[z]
+
+    def partials(c):
+        wait_bytes(hop.at[pl.ds(0, N_Z - 1), :, :, chunks[c]], hopz_sem.at[c, 1])
+        weight = w01[:, :, chunks[c]].reshape(2 * WIDE, CHUNK)
+        for k in (1, 2, 3, 0):
+            g = lax.rem(col + k, N_DP)
+            product = jnp.dot(lhs[g], weight, preferred_element_type=F32)
+            if k:
+                part_send[c, k - 1] = product.astype(BF16)
+                send(part_send.at[c, k - 1], part_got.at[c, k - 1], p_sem.at[c], {"dp": g})
+            else:
+                total[c] = product
+
+    def add_up(c):
+        wait_bytes(part_got.at[c], p_sem.at[c, 1])
+        got = part_got[c].astype(F32)
+        sums[c] = (total[c] + got[0] + got[1] + got[2]).astype(BF16)
+
+    def home_z(c):
+        over_z(
+            lambda peer, there: send(
+                sums.at[c, span(peer * 16, 16), :], bz.at[c, my16, :], bz_sem.at[c], there
+            )
+        )
+        bz[c, my16, :] = sums[c, my16, :]
+
+    def home_yc(c):
+        wait_bytes(bz.at[c, pl.ds(0, 16 * (N_Z - 1)), :], bz_sem.at[c, 1])
+        bp[c] = turn_rows(bz[c], N_YC, N_Z)
+        over_yc(
+            lambda peer, there: send(
+                bp.at[c, span(peer * 32, 32), :], ret.at[c, my32y, :], by_sem.at[c], there
+            )
+        )
+        ret[c, my32y, :] = bp[c, my32y, :]
 
     wait_bytes(hg.at[pl.ds(0, N_DP - 1)], hx_sem.at[1])
     wait_bytes(ogz.at[:, pl.ds(0, 16 * (N_Z - 1)), :], z_sem.at[1])
@@ -244,12 +295,13 @@
             (((0,), (0,)), ((), ())),
             preferred_element_type=F32,
         )
-    for c in range(0, WIDE, 128):
-        gram[c : c + 128, :] = exact(grad[:, c : c + 128].T, grad[...])
-
-    for k in range(1, N_DP):
+
+    for k in (1, 2, 3, 0):
         peer = lax.rem(col + k, N_DP)
-        send(gram.at[span(peer * 128, 128), :], gram_got.at[k - 1], g_sem.at[k - 1], {"dp": peer})
+        block = span(peer * 128, 128)
+        gram[block, :] = exact(grad[:, block].T, grad[...])
+        if k:
+            send(gram.at[block, :], gram_got.at[k - 1], g_sem.at[k - 1], {"dp": peer})
     for g in range(N_DP):
         second = jnp.concatenate([hg[g, :, WIDE:]] * (WIDE // FLAG), axis=1).astype(F32)
         rows = ogz[g].astype(F32)
@@ -277,47 +329,36 @@
     a1 = poly[...] * scale * scale
     q1 = POLY_FIRST * eye + POLY_SECOND * a1 + POLY_THIRD * exact(a1, a1)
     a2 = exact(exact(q1, a1), q1)
+    partials(0)
     q2 = POLY_FIRST * eye + POLY_SECOND * a2 + POLY_THIRD * exact(a2, a2)
     turn[...] = exact(q1, q2) * (scale * (UPDATE_SCALE * (N_DP * WIDE) ** 0.5))
-    upd_ref[...] = exact(grad[...], turn[...])
-
-    wait_bytes(hop.at[pl.ds(0, N_Z - 1)], hopz_sem.at[1])
+    partials(1)
+    add_up(0)
+    updated[...] = exact(grad[...], turn[...])
+    save_update = pltpu.make_async_copy(updated, upd_ref, out_sem.at[0])
+    save_update.start()
+
+    partials(2)
+    add_up(1)
+    partials(3)
+    for c in range(2):
+        home_z(c)
+    add_up(2)
+    home_z(2)
+    moved[...] = w01[0].astype(F32) - LEARNING_RATE * updated[...]
+    save_moved = pltpu.make_async_copy(moved, mov_ref, out_sem.at[1])
+    save_moved.start()
+    add_up(3)
+    home_z(3)
     for c in range(CHUNKS):
-        lanes = pl.ds(c * CHUNK, CHUNK)
-        weight = w01[:, :, lanes].reshape(2 * WIDE, CHUNK)
-        for k in (1, 2, 3, 0):
-            g = lax.rem(col + k, N_DP)
-            product = jnp.dot(lhs[g], weight, preferred_element_type=F32)
-            if k:
-                part_send[c, k - 1] = product.astype(BF16)
-                send(part_send.at[c, k - 1], part_got.at[c, k - 1], p_sem.at[c], {"dp": g})
-            else:
-                total[c] = product
-    for c in range(CHUNKS):
-        wait_bytes(part_got.at[c], p_sem.at[c, 1])
-        got = part_got[c].astype(F32)
-        sums[c] = (total[c] + got[0] + got[1] + got[2]).astype(BF16)
-        over_z(
-            lambda peer, there: send(
-                sums.at[c, span(peer * 16, 16), :], bz.at[c, my16, :], bz_sem.at[c], there
-            )
-        )
-        bz[c, my16, :] = sums[c, my16, :]
-    mov_ref[...] = w01[0].astype(F32) - LEARNING_RATE * upd_ref[...]
-    for c in range(CHUNKS):
-        wait_bytes(bz.at[c, pl.ds(0, 16 * (N_Z - 1)), :], bz_sem.at[c, 1])
-        bp[c] = turn_rows(bz[c], N_YC, N_Z)
-        over_yc(
-            lambda peer, there: send(
-                bp.at[c, span(peer * 32, 32), :], ret.at[c, my32y, :], by_sem.at[c], there
-            )
-        )
-        ret[c, my32y, :] = bp[c, my32y, :]
+        home_yc(c)
     for c in range(CHUNKS):
         wait_bytes(ret.at[c, pl.ds(0, 32 * (N_YC - 1)), :], by_sem.at[c, 1])
-        out_ref[:, pl.ds(c * CHUNK, CHUNK)] = lax.dot_general(
+        home[:, chunks[c]] = lax.dot_general(
             back[...], ret[c], (((0,), (0,)), ((), ())), preferred_element_type=F32
         )
+    save_home = pltpu.make_async_copy(home, out_ref, out_sem.at[2])
+    save_home.start()
 
     for c in range(CHUNKS):
         wait_bytes(part_got.at[c], p_sem.at[c, 0])
@@ -326,26 +367,30 @@
     wait_bytes(wz.at[pl.ds(0, N_Z - 1)], wz_sem.at[0])
     wait_bytes(wp.at[pl.ds(0, N_YC - 1)], wy_sem.at[0])
     wait_bytes(pay.at[pl.ds(0, N_YC - 1)], hopy_sem.at[0])
-    wait_bytes(hop.at[pl.ds(0, N_Z - 1)], hopz_sem.at[0])
+    for c in range(CHUNKS):
+        wait_bytes(hop.at[pl.ds(0, N_Z - 1), :, :, chunks[c]], hopz_sem.at[c, 0])
     wait_bytes(ogx.at[pl.ds(0, N_DP - 1)], x_sem.at[0])
     wait_bytes(ogy.at[:, pl.ds(0, 32 * (N_YC - 1)), :], y_sem.at[0])
     wait_bytes(ogz.at[:, pl.ds(0, 16 * (N_Z - 1)), :], z_sem.at[0])
     wait_bytes(hy.at[pl.ds(0, 32 * (N_YC - 1)), :], hy_sem.at[0])
     wait_bytes(hp.at[pl.ds(0, 16 * (N_Z - 1)), :], hz_sem.at[0])
     wait_bytes(hg.at[pl.ds(0, N_DP - 1)], hx_sem.at[0])
+    save_update.wait()
+    save_moved.wait()
+    save_home.wait()
 
 
 def call(kernel, outs, scratch, semaphores, collective_id, *args):
-    vmem = pl.BlockSpec(memory_space=pltpu.VMEM)
+    hbm = pl.BlockSpec(memory_space=pltpu.HBM)
     return pl.pallas_call(
         kernel,
         out_shape=[jax.ShapeDtypeStruct(*o) for o in outs],
-        in_specs=[vmem] * len(args),
-        out_specs=[vmem] * len(outs),
+        in_specs=[hbm] * len(args),
+        out_specs=[hbm] * len(outs),
         scratch_shapes=[pltpu.VMEM(*s) for s in scratch]
         + [pltpu.SemaphoreType.DMA(s) for s in semaphores],
         compiler_params=pltpu.CompilerParams(
-            collective_id=collective_id, has_side_effects=True, vmem_limit_bytes=48 * 2**20
+            collective_id=collective_id, has_side_effects=True, vmem_limit_bytes=58 * 2**20
         ),
     )(*args)
 
@@ -358,6 +403,13 @@
         kernel,
         [((N_EP, WIDE), F32), ((WIDE, WIDE), F32), ((WIDE, WIDE), F32)],
         [
+            ((N_EP, N_DP * WIDE), BF16),
+            ((N_EP, WIDE), BF16),
+            ((WIDE, WIDE), F32),
+            ((4, 1, N_EP), jnp.int32),
+            ((N_EP, WIDE), F32),
+            ((WIDE, WIDE), F32),
+            ((WIDE, WIDE), F32),
             ((WIDE, WIDE), BF16),
             ((N_Z, 32, WIDE), BF16),
             ((N_YC, N_Z, 16, 128), BF16),
@@ -390,7 +442,7 @@
             ((CHUNKS, ROWS, CHUNK), BF16),
             ((CHUNKS, ROWS, CHUNK), BF16),
         ],
-        [(2,)] * 10 + [(3, 2), (2,)] + [(CHUNKS, 2)] * 3,
+        [(2,)] * 3 + [(CHUNKS, 2)] + [(2,)] * 6 + [(3, 2), (2,)] + [(CHUNKS, 2)] * 3 + [(7,), (3,)],
         0,
         out_grads,
         hidden_acts,

time: 182 us -> 175 us (0.962)
  Pallas kernels: 174 us -> 169 us
    pallas_call x1, Pallas kernels: 174 us -> 169 us  [call(): pl.pallas_call(kernel, out_shape=[jax.ShapeDtypeStruct(*o) for o in outs]...]
    unnamed x17 -> x5, local copies, waits for them, and re-layouts: 6.48 us -> 5 us
where the time goes in v1:
time: 175 us; the launch traced here: 174 us
  Pallas kernels  169 us (97%)
  local copies, waits for them, and re-layouts  5 us (3%)
    pallas_call x1, Pallas kernels, call(): pl.pallas_call(kernel, out_shape=[jax.ShapeDtypeStruct(*o) for o in outs]...  169 us
    unnamed x5, local copies, waits for them, and re-layouts  5 us

profile of v1, /device:TPU:1, one launch (start us, length us, event | category | flops | bytes accessed | tf_op | source)
XLA Modules:
  0.0 174.5 jit_solution(11837175887824913241)
XLA Ops:
  0.6 168.8 %shard_map.94 = (f32[128,512]{1,0:T(8,128)}, f32[512,512]{1,0:T(8,128)}, f32[512,512]{1,0:T(8,128)}) custom-call(bf16[128,2048]{1,0:T(8,128)(2,1)} %og_ref.1, bf16[128,512]{1,0:T(8,128)(2,1)} %ha_ref.1, s32[1,128]{1,0:T(1,128)} %bitcast.10, s32[1,128]{1,0:T(1,128)} %bitcast.11, f32[512,512]{1,0:T(8,128)} %bitcast.7, s32[1,128]{1,0:T(1,128)} %bitcast.12, ...), custom_call_target="tpu_custom_call" | custom-call | tf_op jit(solution)/shard_map/pallas_call | solution.py:385
  169.5 1.7 copy.13
  171.2 0.0 copy-start
  171.2 2.4 %copy.14 = f32[1,512,512]{2,1,0:T(8,128)} copy(f32[1,512,512]{2,1,0:T(8,128)} %bitcast.9) | data formatting | bytes 2097152
  173.5 0.0 copy-done
  173.5 1.0 copy.15
Async XLA Ops:
  171.2 2.4 %copy-start = (f32[512,512]{1,0:T(8,128)S(1)}, f32[512,512]{1,0:T(8,128)}, u32[]{:S(2)}) copy-start(f32[512,512]{1,0:T(8,128)} %get-tuple-element.8) | copy-start | bytes 3145732

commit v2 on v1

--- a/solution.py
+++ b/solution.py
@@ -121,12 +121,12 @@
 
 def kernel(
     og_ref, ha_ref, named_ref, pick_ref, weight_ref, now_ref, next_ref,
-    out_ref, mov_ref, upd_ref,
-    og_in, ha_in, weight_in, tables, home, moved, updated,
-    wb, wz, wp, wide, chosen, pay, hop, w01,
-    ogs, ogx, ogy, ogp, ogz, has, hy, hp, hg, back,
+    ret, back, w01, upd_ref,
+    og_in, ha_in, weight_in, tables, updated,
+    wb, wz, wp, wide, chosen, pay, hop,
+    ogs, ogx, ogy, ogp, ogz, has, hy, hp, hg,
     lhs, grad, gram, gram_got, poly, turn,
-    part_send, part_got, total, sums, bz, bp, ret,
+    part_send, part_got, total, sums, bz, bp,
     wz_sem, wy_sem, hopy_sem, hopz_sem, x_sem, y_sem, z_sem, hy_sem, hz_sem, hx_sem,
     g_sem, a_sem, p_sem, bz_sem, by_sem, in_sem, out_sem,
 ):
@@ -280,10 +280,10 @@
         bp[c] = turn_rows(bz[c], N_YC, N_Z)
         over_yc(
             lambda peer, there: send(
-                bp.at[c, span(peer * 32, 32), :], ret.at[c, my32y, :], by_sem.at[c], there
+                bp.at[c, span(peer * 32, 32), :], ret.at[my32y, chunks[c]], by_sem.at[c], there
             )
         )
-        ret[c, my32y, :] = bp[c, my32y, :]
+        ret[my32y, chunks[c]] = bp[c, my32y, :]
 
     wait_bytes(hg.at[pl.ds(0, N_DP - 1)], hx_sem.at[1])
     wait_bytes(ogz.at[:, pl.ds(0, 16 * (N_Z - 1)), :], z_sem.at[1])
@@ -335,7 +335,7 @@
     partials(1)
     add_up(0)
     updated[...] = exact(grad[...], turn[...])
-    save_update = pltpu.make_async_copy(updated, upd_ref, out_sem.at[0])
+    save_update = pltpu.make_async_copy(updated, upd_ref, out_sem)
     save_update.start()
 
     partials(2)
@@ -345,25 +345,17 @@
         home_z(c)
     add_up(2)
     home_z(2)
-    moved[...] = w01[0].astype(F32) - LEARNING_RATE * updated[...]
-    save_moved = pltpu.make_async_copy(moved, mov_ref, out_sem.at[1])
-    save_moved.start()
     add_up(3)
     home_z(3)
     for c in range(CHUNKS):
         home_yc(c)
     for c in range(CHUNKS):
-        wait_bytes(ret.at[c, pl.ds(0, 32 * (N_YC - 1)), :], by_sem.at[c, 1])
-        home[:, chunks[c]] = lax.dot_general(
-            back[...], ret[c], (((0,), (0,)), ((), ())), preferred_element_type=F32
-        )
-    save_home = pltpu.make_async_copy(home, out_ref, out_sem.at[2])
-    save_home.start()
+        wait_bytes(ret.at[pl.ds(0, 32 * (N_YC - 1)), chunks[c]], by_sem.at[c, 1])
 
     for c in range(CHUNKS):
         wait_bytes(part_got.at[c], p_sem.at[c, 0])
         wait_bytes(bz.at[c, pl.ds(0, 16 * (N_Z - 1)), :], bz_sem.at[c, 0])
-        wait_bytes(ret.at[c, pl.ds(0, 32 * (N_YC - 1)), :], by_sem.at[c, 0])
+        wait_bytes(ret.at[pl.ds(0, 32 * (N_YC - 1)), chunks[c]], by_sem.at[c, 0])
     wait_bytes(wz.at[pl.ds(0, N_Z - 1)], wz_sem.at[0])
     wait_bytes(wp.at[pl.ds(0, N_YC - 1)], wy_sem.at[0])
     wait_bytes(pay.at[pl.ds(0, N_YC - 1)], hopy_sem.at[0])
@@ -376,17 +368,16 @@
     wait_bytes(hp.at[pl.ds(0, 16 * (N_Z - 1)), :], hz_sem.at[0])
     wait_bytes(hg.at[pl.ds(0, N_DP - 1)], hx_sem.at[0])
     save_update.wait()
-    save_moved.wait()
-    save_home.wait()
 
 
 def call(kernel, outs, scratch, semaphores, collective_id, *args):
+    vmem = pl.BlockSpec(memory_space=pltpu.VMEM)
     hbm = pl.BlockSpec(memory_space=pltpu.HBM)
     return pl.pallas_call(
         kernel,
         out_shape=[jax.ShapeDtypeStruct(*o) for o in outs],
         in_specs=[hbm] * len(args),
-        out_specs=[hbm] * len(outs),
+        out_specs=[vmem] * (len(outs) - 1) + [hbm],
         scratch_shapes=[pltpu.VMEM(*s) for s in scratch]
         + [pltpu.SemaphoreType.DMA(s) for s in semaphores],
         compiler_params=pltpu.CompilerParams(
@@ -399,16 +390,19 @@
     out_grads, hidden_acts, routing, replica_pick, master_weights, current_slots, next_slots
 ):
     wide_acts = WIDE + FLAG
-    input_grads, moved_weight, update = call(
+    returned, back, moved, update = call(
         kernel,
-        [((N_EP, WIDE), F32), ((WIDE, WIDE), F32), ((WIDE, WIDE), F32)],
+        [
+            ((ROWS, WIDE), BF16),
+            ((ROWS, N_EP), BF16),
+            ((2, WIDE, WIDE), BF16),
+            ((WIDE, WIDE), F32),
+        ],
         [
             ((N_EP, N_DP * WIDE), BF16),
             ((N_EP, WIDE), BF16),
             ((WIDE, WIDE), F32),
             ((4, 1, N_EP), jnp.int32),
-            ((N_EP, WIDE), F32),
-            ((WIDE, WIDE), F32),
             ((WIDE, WIDE), F32),
             ((WIDE, WIDE), BF16),
             ((N_Z, 32, WIDE), BF16),
@@ -417,7 +411,6 @@
             ((ROWS * 16, 128), F32),
             ((N_YC, N_Z, 2, 16, 128), BF16),
             ((N_Z, 2, 32, WIDE), BF16),
-            ((2, WIDE, WIDE), BF16),
             ((ROWS, N_DP * WIDE), BF16),
             ((N_DP, ROWS, WIDE), BF16),
             ((N_DP, ROWS, WIDE), BF16),
@@ -427,7 +420,6 @@
             ((ROWS, wide_acts), BF16),
             ((ROWS, wide_acts), BF16),
             ((N_DP, ROWS, wide_acts), BF16),
-            ((ROWS, N_EP), BF16),
             ((N_DP, ROWS, 2 * WIDE), BF16),
             ((WIDE, WIDE), F32),
             ((WIDE, WIDE), F32),
@@ -440,9 +432,8 @@
             ((CHUNKS, ROWS, CHUNK), BF16),
             ((CHUNKS, ROWS, CHUNK), BF16),
             ((CHUNKS, ROWS, CHUNK), BF16),
-            ((CHUNKS, ROWS, CHUNK), BF16),
         ],
-        [(2,)] * 3 + [(CHUNKS, 2)] + [(2,)] * 6 + [(3, 2), (2,)] + [(CHUNKS, 2)] * 3 + [(7,), (3,)],
+        [(2,)] * 3 + [(CHUNKS, 2)] + [(2,)] * 6 + [(3, 2), (2,)] + [(CHUNKS, 2)] * 3 + [(7,), ()],
         0,
         out_grads,
         hidden_acts,
@@ -452,6 +443,10 @@
         current_slots.reshape(1, N_EP),
         next_slots.reshape(1, N_EP),
     )
+    input_grads = lax.dot_general(
+        back, returned, (((0,), (0,)), ((), ())), preferred_element_type=F32
+    )
+    moved_weight = moved[0].astype(F32) - LEARNING_RATE * update
     return (input_grads, moved_weight[None], update[None])
 
 

time: 175 us -> 175 us (level)
  local copies, waits for them, and re-layouts: 5 us -> 0.97 us
  other arithmetic: 0 us -> 2.58 us
  matrix products: 0 us -> 1.9 us
    unnamed x5 -> x3, local copies, waits for them, and re-layouts: 5 us -> 0.97 us
    broadcast_in_dim x0 -> x1, other arithmetic: none -> 2.58 us  [per_device(): return (input_grads, moved_weight[None], update[None])]
    dot_general x0 -> x1, matrix products: none -> 1.9 us  [per_device(): lax.dot_general(back, returned, (((0,), (0,)), ((), ())), preferred_eleme...]
where the time goes in v2:
time: 175 us
  Pallas kernels  169 us (97%)
  other arithmetic  2.58 us (1%)
  matrix products  1.9 us (1%)
    pallas_call x1, Pallas kernels, call(): pl.pallas_call(kernel, out_shape=[jax.ShapeDtypeStruct(*o) for o in outs]...  169 us

profile of v2, /device:TPU:1, one launch (start us, length us, event | category | flops | bytes accessed | tf_op | source)
XLA Modules:
  0.0 175.2 jit_solution(4379613759262192945)
XLA Ops:
  0.6 169.1 %shard_map.94 = (bf16[256,512]{1,0:T(8,128)(2,1)}, bf16[256,128]{1,0:T(8,128)(2,1)}, bf16[2,512,512]{2,1,0:T(8,128)(2,1)}, f32[512,512]{1,0:T(8,128)}) custom-call(bf16[128,2048]{1,0:T(8,128)(2,1)} %og_ref.1, bf16[128,512]{1,0:T(8,128)(2,1)} %ha_ref.1, s32[1,128]{1,0:T(1,128)} %bitcast.15, s32[1,128]{1,0:T(1,128)} %bitcast.16, f32[512,512]{1,0:T(8,128)} %bitcast.14, ...), custom_call_target="tpu_custom_call" | custom-call | tf_op jit(solution)/shard_map/pallas_call | solution.py:376
  169.7 1.9 %fusion.1 = f32[128,512]{1,0:T(8,128)} fusion(bf16[256,128]{1,0:T(8,128)(2,1)} %get-tuple-element.7, bf16[256,512]{1,0:T(8,128)(2,1)} %get-tuple-element.8), kind=kOutput, calls=%fused_computation.2 | convolution fusion | flops 33554432 | bytes 589824 | tf_op jit(solution)/shard_map/dot_general | solution.py:446
  171.6 0.0 copy-start
  171.6 2.6 %fusion = f32[1,512,512]{2,1,0:T(8,128)} fusion(f32[512,512]{1,0:T(8,128)} %get-tuple-element.10, bf16[2,512,512]{2,1,0:T(8,128)(2,1)} %get-tuple-element.9), kind=kLoop, calls=%fused_computation.1 | loop fusion | flops 786432 | bytes 2621440 | tf_op jit(solution)/shard_map/broadcast_in_dim | solution.py:450
  174.2 0.0 copy-done
  174.2 1.0 copy.11
Async XLA Ops:
  171.6 2.6 %copy-start = (f32[512,512]{1,0:T(8,128)S(1)}, f32[512,512]{1,0:T(8,128)}, u32[]{:S(2)}) copy-start(f32[512,512]{1,0:T(8,128)} %get-tuple-element.10) | copy-start | bytes 3145732

commit v3 on v1

--- a/solution.py
+++ b/solution.py
@@ -22,7 +22,7 @@
 ROWS = 2 * N_EP
 WIDE = 512
 FLAG = 128
-CHUNKS = 4
+CHUNKS = 2
 CHUNK = WIDE // CHUNKS
 
 
@@ -329,27 +329,21 @@
     a1 = poly[...] * scale * scale
     q1 = POLY_FIRST * eye + POLY_SECOND * a1 + POLY_THIRD * exact(a1, a1)
     a2 = exact(exact(q1, a1), q1)
-    partials(0)
     q2 = POLY_FIRST * eye + POLY_SECOND * a2 + POLY_THIRD * exact(a2, a2)
     turn[...] = exact(q1, q2) * (scale * (UPDATE_SCALE * (N_DP * WIDE) ** 0.5))
-    partials(1)
-    add_up(0)
+    partials(0)
     updated[...] = exact(grad[...], turn[...])
     save_update = pltpu.make_async_copy(updated, upd_ref, out_sem.at[0])
     save_update.start()
 
-    partials(2)
-    add_up(1)
-    partials(3)
-    for c in range(2):
-        home_z(c)
-    add_up(2)
-    home_z(2)
+    add_up(0)
+    partials(1)
+    home_z(0)
     moved[...] = w01[0].astype(F32) - LEARNING_RATE * updated[...]
     save_moved = pltpu.make_async_copy(moved, mov_ref, out_sem.at[1])
     save_moved.start()
-    add_up(3)
-    home_z(3)
+    add_up(1)
+    home_z(1)
     for c in range(CHUNKS):
         home_yc(c)
     for c in range(CHUNKS):

time: 175 us -> 177 us (1.011)
  Pallas kernels: 169 us -> 171 us
    pallas_call x1, Pallas kernels: 169 us -> 171 us  [call(): pl.pallas_call(kernel, out_shape=[jax.ShapeDtypeStruct(*o) for o in outs]...]
where the time goes in v3:
time: 177 us
  Pallas kernels  171 us (97%)
  local copies, waits for them, and re-layouts  5 us (3%)
    pallas_call x1, Pallas kernels, call(): pl.pallas_call(kernel, out_shape=[jax.ShapeDtypeStruct(*o) for o in outs]...  171 us
    unnamed x5, local copies, waits for them, and re-layouts  5 us

profile of v3, /device:TPU:1, one launch (start us, length us, event | category | flops | bytes accessed | tf_op | source)
XLA Modules:
  0.0 176.7 jit_solution(3280058923014005570)
XLA Ops:
  0.6 171.1 %shard_map.94 = (f32[128,512]{1,0:T(8,128)}, f32[512,512]{1,0:T(8,128)}, f32[512,512]{1,0:T(8,128)}) custom-call(bf16[128,2048]{1,0:T(8,128)(2,1)} %og_ref.1, bf16[128,512]{1,0:T(8,128)(2,1)} %ha_ref.1, s32[1,128]{1,0:T(1,128)} %bitcast.10, s32[1,128]{1,0:T(1,128)} %bitcast.11, f32[512,512]{1,0:T(8,128)} %bitcast.7, s32[1,128]{1,0:T(1,128)} %bitcast.12, ...), custom_call_target="tpu_custom_call" | custom-call | tf_op jit(solution)/shard_map/pallas_call | solution.py:379
  171.7 1.7 copy.13
  173.4 0.0 copy-start
  173.4 2.4 %copy.14 = f32[1,512,512]{2,1,0:T(8,128)} copy(f32[1,512,512]{2,1,0:T(8,128)} %bitcast.9) | data formatting | bytes 2097152
  175.7 0.0 copy-done
  175.7 1.0 copy.15
Async XLA Ops:
  173.4 2.4 %copy-start = (f32[512,512]{1,0:T(8,128)S(1)}, f32[512,512]{1,0:T(8,128)}, u32[]{:S(2)}) copy-start(f32[512,512]{1,0:T(8,128)} %get-tuple-element.8) | copy-start | bytes 3145732
